TPU v7x, 32 devices: a whole 2x2x4 slice. The times are simulated.
32 devices in a mesh: real: 2 (over x), up: 8 (over z, y), dn: 2 (over core).
Axes of the slice: x: 2, y: 2, z: 4, core: 2. Of those that a mesh axis runs over, the one named last changes fastest.
Arguments:
- start: float32 [6, 2048, 2048], P('real', 'up', 'dn'), parts along dimension 0, may hold values from -700 to 700
- up_occupied: int32 [2048, 14], P('up'), may hold values 0 or 1
- dn_occupied: int32 [2048, 14], P('dn'), may hold values 0 or 1
- disorder: float32 [28], P('real'), parts along dimension 0, may hold values from -1.5 to 1.5
- hop_tiles: float32 [16, 128, 128], replicated, may hold values from -0.15625 to 0.15625
- up_index: int32 [16, 5], replicated, may hold values from 0 to 15
- dn_index: int32 [16, 5], replicated, may hold values from 0 to 15
Outputs:
- filtered: float32 [6, 2048, 2048], P('real', 'up', 'dn'), parts along dimension 0
- gram: float32 [4, 3, 3], P('real'), parts along dimension 0
There are 2 independent parts, one for each index of `real`. A program takes and returns all parts, laid end to end along the dimension named above; an argument that names none is the same for every part. Nothing has to cross between parts.
All inputs are finite; a program needn't handle non-finite values. No bound on the sum of `up_occupied` or of `dn_occupied` on one device may be relied on, other than what follows from the above.
Results may differ from a plain program's by a relative error of at most 0.0001.
Values sent between devices are 32-bit elements; how exact they have to be, the bound alone decides.
A program may use at most 192 MiB of HBM per device.

v0:
```python
import jax
import jax.numpy as jnp
import numpy as np
from jax import lax
from jax.sharding import PartitionSpec as P

highest = lax.Precision.HIGHEST


def swapped(block, axis, bit):
    count = lax.axis_size(axis)
    route = []
    for low in range(count):
        high = low | 1 << bit
        if high != low and high < count:
            route += [(low, high), (high, low)]
    return lax.ppermute(block, axis, route)


def pair_tiles(bank, table, rows, bit):
    others = rows ^ 1 << bit
    lower = jnp.minimum(rows, others)
    picked = bank[table[lower, bit + 1]]
    flipped = jnp.swapaxes(picked, 1, 2)
    return jnp.where((rows < others)[:, None, None], picked, flipped)


def own_tiles(bank, table, rows):
    picked = bank[table[rows, 0]]
    return 0.5 * (picked + jnp.swapaxes(picked, 1, 2))


def row_terms(blocks, rows, bank, table):
    total = jnp.einsum("jab,vjbc->vjac", own_tiles(bank, table, rows), blocks, precision=highest)
    partner = np.arange(blocks.shape[1]) ^ 1 << 0
    total = total + jnp.einsum(
        "jab,vjbc->vjac", pair_tiles(bank, table, rows, 0), blocks[:, partner], precision=highest
    )
    return total


def column_terms(blocks, rows, bank, table, local_bits):
    total = jnp.einsum("jab,vujb->vuja", own_tiles(bank, table, rows), blocks, precision=highest)
    for bit in range(local_bits):
        partner = np.arange(blocks.shape[2]) ^ 1 << bit
        total = total + jnp.einsum(
            "jab,vujb->vuja",
            pair_tiles(bank, table, rows, bit),
            blocks[:, :, partner],
            precision=highest,
        )
    return total


def up_swapped(field, bank, table):
    width = bank.shape[1]
    local = field.shape[1] // width
    local_bits = local.bit_length() - 1
    rows = lax.axis_index("up") * local + jnp.arange(local, dtype=jnp.int32)
    shape = (field.shape[0], local, width, field.shape[2])
    total = row_terms(field.reshape(shape), rows, bank, table)
    for level in range(lax.axis_size("up").bit_length() - 1):
        other = swapped(field, "up", level)
        tiles = pair_tiles(bank, table, rows, local_bits + level)
        total = total + jnp.einsum("jab,vjbc->vjac", tiles, other.reshape(shape), precision=highest)
    return total.reshape(field.shape)


def dn_swapped(field, bank, table):
    width = bank.shape[1]
    local = field.shape[2] // width
    local_bits = local.bit_length() - 1
    rows = lax.axis_index("dn") * local + jnp.arange(local, dtype=jnp.int32)
    shape = (field.shape[0], field.shape[1], local, width)
    total = column_terms(field.reshape(shape), rows, bank, table, local_bits)
    other = swapped(field, "dn", 0)
    tiles = pair_tiles(bank, table, rows, local_bits)
    total = total + jnp.einsum("jab,vujb->vuja", tiles, other.reshape(shape), precision=highest)
    return total.reshape(field.shape)


def operate(field, potential, bank, up_table, dn_table, shift):
    up_part = up_swapped(field, bank, up_table)
    dn_part = dn_swapped(field, bank, dn_table)
    return up_part + dn_part + (potential - shift)[None] * field


def body(start, up_occupied, dn_occupied, disorder, hop_tiles, up_index, dn_index):
    up_float = up_occupied.astype(jnp.float32)
    dn_float = dn_occupied.astype(jnp.float32)
    potential = jnp.dot(up_float, dn_float.T, precision=highest)
    potential = potential + jnp.dot(up_float, disorder, precision=highest)[:, None]
    potential = potential + jnp.dot(dn_float, disorder, precision=highest)[None, :]
    shift = 0.25 * up_occupied.shape[1]
    cells = start.shape[1] * start.shape[2] * lax.axis_size("up") * lax.axis_size("dn")
    first = operate(start, potential, hop_tiles, up_index, dn_index, shift)
    second = operate(first, potential, hop_tiles, up_index, dn_index, shift)
    correlation, image = lax.psum(
        (
            jnp.einsum("vud,wud->vw", first, first, precision=highest),
            jnp.einsum("vud,wud->vw", first, second, precision=highest),
        ),
        ("up", "dn"),
    )
    scale = jnp.sqrt(jnp.diagonal(correlation) / cells + 1e-06)
    outer = scale[:, None] * scale[None, :]
    gram = jnp.stack([correlation / outer, image / outer]) / cells
    return (second / scale[:, None, None], gram)


def solution(mesh):
    return jax.shard_map(
        body,
        mesh=mesh,
        in_specs=(P("real", "up", "dn"), P("up", None), P("dn", None), P("real"), P(), P(), P()),
        out_specs=(P("real", "up", "dn"), P("real", None, None)),
        check_vma=False,
    )
```

profile of v0, /device:TPU:0, one launch (start us, length us, event | category | flops | bytes accessed | tf_op | source)
XLA Modules:
  0.0 402.1 jit_solution(2026373222081302727)
XLA Ops:
  0.7 3.1 collective-permute-start.1
  5.3 2.6 collective-permute-start.2
  7.9 3.6 copy.135
  21.3 6.5 %fusion.21 = f32[8,128,3,256]{3,1,2,0:T(8,128)} fusion(f32[3,256,8,128]{1,3,2,0:T(8,128)} %bitcast.334, f32[8,128,128]{1,2,0:T(8,128)S(1)} %copy.134, f32[8,128,128]{2,1,0:T(8,128)S(1)} %gather_fusion.12), kind=kOutput, calls=%fused_computation.55 | convolution fusion | flops 1208221696 | bytes 7340032 | tf_op jit(solution)/shard_map/jab,vujb->vuja/dot_general | solution.py:43
  27.8 4.5 %fusion.40 = f32[2,128,3,1024]{3,1,2,0:T(8,128)} fusion(f32[3,2,128,1024]{3,2,1,0:T(8,128)S(1)} %bitcast.333, f32[2,128,128]{1,2,0:T(8,128)S(1)} %copy.119, f32[2,128,128]{2,1,0:T(8,128)S(1)} %gather_fusion.1), kind=kOutput, calls=%fused_computation.79 | convolution fusion | flops 1208025088 | bytes 6553600 | tf_op jit(solution)/shard_map/jab,vjbc->vjac/dot_general | solution.py:34
  35.6 3.9 copy.138
  41.1 4.3 %gather_fusion.19 = f32[8,3,256,128]{3,2,1,0:T(8,128)} fusion(f32[3,256,8,128]{3,1,2,0:T(8,128)} %copy.138, s32[1024]{0:T(1024)S(1)} %pad_clamp_fusion.2), kind=kCustom, calls=%fused_computation.19 | custom fusion | bytes 6291488 | tf_op jit(solution)/shard_map/gather | solution.py:49
  45.5 4.3 %gather_fusion.16 = f32[8,3,256,128]{3,2,1,0:T(8,128)} fusion(f32[3,256,8,128]{3,1,2,0:T(8,128)} %copy.138, s32[1024]{0:T(1024)S(1)} %pad_clamp_fusion.4), kind=kCustom, calls=%fused_computation.16 | custom fusion | bytes 6291488 | tf_op jit(solution)/shard_map/gather | solution.py:49
  51.4 4.3 %gather_fusion.13 = f32[8,3,256,128]{3,2,1,0:T(8,128)} fusion(f32[3,256,8,128]{3,1,2,0:T(8,128)} %copy.138, s32[1024]{0:T(1024)S(1)} %pad_clamp_fusion.6), kind=kCustom, calls=%fused_computation.13 | custom fusion | bytes 6291488 | tf_op jit(solution)/shard_map/gather | solution.py:49
  61.5 4.3 %gather_fusion.2 = f32[2,3,128,1024]{3,2,1,0:T(8,128)} fusion(f32[3,2,128,1024]{3,2,1,0:T(8,128)} %bitcast.332, s32[1024]{0:T(1024)S(1)} %pad_clamp_fusion.12), kind=kCustom, calls=%fused_computation.2 | custom fusion | bytes 6291464 | tf_op jit(solution)/shard_map/gather | solution.py:37
  68.5 5.4 %fusion.24 = f32[2,3,1024,128]{2,3,1,0:T(8,128)S(1)} fusion(f32[2,3,128,1024]{3,2,1,0:T(8,128)} %gather_fusion.2, f32[2,128,128]{1,2,0:T(8,128)} %copy.122, f32[2,128,128]{2,1,0:T(8,128)} %copy-done.44, pred[2]{0:T(512)(128)(4,1)} %get-tuple-element.23), kind=kOutput, calls=%fused_computation.63 | convolution fusion | flops 1207992320 | bytes 6553602 | tf_op jit(solution)/shard_map/jab,vjbc->vjac/dot_general | solution.py:36
  74.0 3.2 fusion.15
  77.3 3.2 fusion.17
  80.6 16.7 %fusion.19 = f32[8,3,256,128]{2,3,1,0:T(8,128)S(1)} fusion(f32[8,3,256,128]{3,2,1,0:T(8,128)S(1)} %copy-done.15, f32[8,128,128]{1,2,0:T(8,128)S(1)} %copy-done.37, f32[8,128,128]{2,1,0:T(8,128)S(1)} %copy-done.28, pred[8]{0:T(512)(128)(4,1)S(1)} %copy-done.65), kind=kOutput, calls=%fused_computation.53 | convolution fusion | flops 1208090624 | bytes 7340040 | tf_op jit(solution)/shard_map/jab,vujb->vuja/dot_general | solution.py:46
  97.4 5.9 %bitcast_add_fusion.1 = f32[3,256,8,128]{1,3,0,2:T(8,128)S(1)} fusion(f32[8,3,256,128]{2,3,1,0:T(8,128)S(1)} %fusion.15, f32[8,3,256,128]{2,3,1,0:T(8,128)S(1)} %fusion.17, f32[8,3,256,128]{2,3,1,0:T(8,128)S(1)} %fusion.19, f32[8,128,3,256]{3,1,2,0:T(8,128)S(1)} %copy-done.17, f32[3,256,8,128]{1,3,2,0:T(8,128)} %bitcast.69, ...), kind=kOutput, calls=%fused_computation.43 | convolution fusion | flops 1211236352 | bytes 19922952 | tf_op jit(solution)/shard_map/jab,vujb->vuja/dot_general | solution.py:78
  105.3 3.7 copy.152
  109.0 29.3 %collective-permute-done.1 = f32[3,256,1024]{2,1,0:T(8,128)} collective-permute-done((f32[3,256,1024]{2,1,0:T(8,128)}, f32[3,256,1024]{2,1,0:T(8,128)}, u32[]{:S(2)}, u32[]{:S(2)}) %collective-permute-start.1) | collective-permute-done | bytes 3145760 | tf_op jit(solution)/shard_map/ppermute | solution.py:17
  138.3 5.2 %fusion.36 = f32[2,128,3,1024]{3,1,2,0:T(8,128)S(1)} fusion(f32[3,2,128,1024]{3,2,1,0:T(8,128)} %bitcast.26, f32[2,128,128]{1,2,0:T(8,128)} %copy.127, f32[2,128,128]{2,1,0:T(8,128)} %copy-done.42, pred[2]{0:T(512)(128)(4,1)} %get-tuple-element.21), kind=kOutput, calls=%fused_computation.75 | convolution fusion | flops 1207992320 | bytes 6553602 | tf_op jit(solution)/shard_map/jab,vjbc->vjac/dot_general | solution.py:65
  143.5 5.1 %fusion.38 = f32[2,128,3,1024]{3,1,2,0:T(8,128)S(1)} fusion(f32[3,2,128,1024]{3,2,1,0:T(8,128)} %bitcast.19, f32[2,128,128]{1,2,0:T(8,128)S(1)} %copy-done.50, f32[2,128,128]{2,1,0:T(8,128)S(1)} %gather_fusion.6, pred[2]{0:T(512)(128)(4,1)S(1)} %copy-done.59), kind=kOutput, calls=%fused_computation.77 | convolution fusion | flops 1207992320 | bytes 6553602 | tf_op jit(solution)/shard_map/jab,vjbc->vjac/dot_general | solution.py:65
  148.6 6.0 %bitcast_add_fusion.6 = f32[3,2,128,1024]{3,2,0,1:T(8,128)S(1)} fusion(f32[2,128,3,1024]{3,1,2,0:T(8,128)S(1)} %fusion.36, f32[2,128,3,1024]{3,1,2,0:T(8,128)S(1)} %fusion.38, f32[2,3,1024,128]{2,3,1,0:T(8,128)S(1)} %fusion.24, f32[2,128,3,1024]{3,1,2,0:T(8,128)S(1)} %copy-done.8, f32[3,2,128,1024]{3,2,1,0:T(8,128)} %bitcast.33, ...), kind=kOutput, calls=%fused_computation.59 | convolution fusion | flops 1211138048 | bytes 19136514 | tf_op jit(solution)/shard_map/jab,vjbc->vjac/dot_general | solution.py:65
  158.7 2.4 copy.163
  161.1 3.5 copy.166
  164.6 4.3 %gather_fusion.27 = f32[8,3,256,128]{3,2,1,0:T(8,128)} fusion(f32[3,256,8,128]{3,1,2,0:T(8,128)} %copy.166, s32[1024]{0:T(1024)S(1)} %pad_clamp_fusion.2), kind=kCustom, calls=%fused_computation.27 | custom fusion | bytes 6291488 | tf_op jit(solution)/shard_map/gather | solution.py:49
  168.9 4.3 %gather_fusion.26 = f32[8,3,256,128]{3,2,1,0:T(8,128)} fusion(f32[3,256,8,128]{3,1,2,0:T(8,128)} %copy.166, s32[1024]{0:T(1024)S(1)} %pad_clamp_fusion.4), kind=kCustom, calls=%fused_computation.26 | custom fusion | bytes 6291488 | tf_op jit(solution)/shard_map/gather | solution.py:49
  173.1 4.4 %gather_fusion.25 = f32[8,3,256,128]{3,2,1,0:T(8,128)} fusion(f32[3,256,8,128]{3,1,2,0:T(8,128)} %copy.166, s32[1024]{0:T(1024)S(1)} %pad_clamp_fusion.6), kind=kCustom, calls=%fused_computation.25 | custom fusion | bytes 6291488 | tf_op jit(solution)/shard_map/gather | solution.py:49
  177.5 2.7 collective-permute-start.4
  180.2 3.0 collective-permute-start.6
  183.2 3.6 copy.177
  186.9 2.7 gather_fusion.24
  189.5 7.0 %fusion.2 = f32[8,3,256,128]{2,3,1,0:T(8,128)} fusion(f32[8,3,256,128]{3,2,1,0:T(8,128)} %gather_fusion.27, f32[8,128,128]{1,2,0:T(8,128)} %copy.145, f32[8,128,128]{2,1,0:T(8,128)} %copy-done.30, pred[8]{0:T(512)(128)(4,1)S(1)} %copy-done.64), kind=kOutput, calls=%fused_computation.31 | convolution fusion | flops 1208090624 | bytes 7340040 | tf_op jit(solution)/shard_map/jab,vujb->vuja/dot_general | solution.py:46
  196.6 4.6 %fusion.8 = f32[8,3,256,128]{2,3,1,0:T(8,128)} fusion(f32[3,256,8,128]{1,3,2,0:T(8,128)S(1)} %bitcast.337, f32[8,128,128]{1,2,0:T(8,128)S(1)} %copy-done.33, f32[8,128,128]{2,1,0:T(8,128)S(1)} %copy-done.21), kind=kOutput, calls=%fused_computation.37 | convolution fusion | flops 1208221696 | bytes 7340032 | tf_op jit(solution)/shard_map/jab,vujb->vuja/dot_general | solution.py:43
  201.3 4.9 %fusion.11 = f32[2,3,1024,128]{2,3,1,0:T(8,128)} fusion(f32[2,3,128,1024]{3,2,1,0:T(8,128)S(1)} %copy-done.16, f32[2,128,128]{1,2,0:T(8,128)S(1)} %copy-done.52, f32[2,128,128]{2,1,0:T(8,128)S(1)} %copy-done.45, pred[2]{0:T(512)(128)(4,1)S(1)} %copy-done.62), kind=kOutput, calls=%fused_computation.41 | convolution fusion | flops 1207992320 | bytes 6553602 | tf_op jit(solution)/shard_map/jab,vjbc->vjac/dot_general | solution.py:36
  206.2 5.2 %fusion.32 = f32[2,3,1024,128]{2,3,1,0:T(8,128)} fusion(f32[3,2,128,1024]{3,2,1,0:T(8,128)S(1)} %bitcast.331, f32[2,128,128]{1,2,0:T(8,128)S(1)} %copy-done.49, f32[2,128,128]{2,1,0:T(8,128)S(1)} %gather_fusion.1), kind=kOutput, calls=%fused_computation.71 | convolution fusion | flops 1208025088 | bytes 6553600 | tf_op jit(solution)/shard_map/jab,vjbc->vjac/dot_general | solution.py:34
  211.4 4.7 %fusion.4 = f32[8,3,256,128]{2,3,1,0:T(8,128)} fusion(f32[8,3,256,128]{3,2,1,0:T(8,128)S(1)} %copy-done.12, f32[8,128,128]{1,2,0:T(8,128)S(1)} %copy-done.36, f32[8,128,128]{2,1,0:T(8,128)S(1)} %copy-done.26, pred[8]{0:T(512)(128)(4,1)S(1)} %copy-done.68), kind=kOutput, calls=%fused_computation.33 | convolution fusion | flops 1208090624 | bytes 7340040 | tf_op jit(solution)/shard_map/jab,vujb->vuja/dot_general | solution.py:46
  216.2 4.8 %fusion.6 = f32[8,3,256,128]{2,3,1,0:T(8,128)} fusion(f32[8,3,256,128]{3,2,1,0:T(8,128)S(1)} %copy-done.11, f32[8,128,128]{1,2,0:T(8,128)S(1)} %copy-done.38, f32[8,128,128]{2,1,0:T(8,128)S(1)} %copy-done.29, pred[8]{0:T(512)(128)(4,1)S(1)} %copy-done.66), kind=kOutput, calls=%fused_computation.35 | convolution fusion | flops 1208090624 | bytes 7340040 | tf_op jit(solution)/shard_map/jab,vujb->vuja/dot_general | solution.py:46
  221.0 19.2 %convolution_bitcast_fusion.1 = f32[3,3]{1,0:T(4,128)S(1)} fusion(f32[3,256,1024]{1,0,2:T(4,128)S(1)} %copy-done.4), kind=kOutput, calls=%fused_computation.88 | convolution fusion | flops 28311552 | bytes 3145764 | tf_op jit(solution)/shard_map/vud,wud->vw/dot_general | solution.py:100
  240.1 3.6 copy.172
  243.7 9.6 %add_bitcast_fusion = f32[3,256,8,128]{1,3,0,2:T(8,128)S(1)} fusion(f32[8,3,256,128]{2,3,1,0:T(8,128)} %fusion.2, f32[8,3,256,128]{2,3,1,0:T(8,128)} %fusion.4, f32[8,3,256,128]{2,3,1,0:T(8,128)} %fusion.8, f32[8,3,256,128]{2,3,1,0:T(8,128)} %fusion.6, f32[3,256,8,128]{1,3,2,0:T(8,128)} %bitcast.340, f32[8,128,128]{1,2,0:T(8,128)} %copy.147, ...), kind=kOutput, calls=%fused_computation.81 | convolution fusion | flops 1211236352 | bytes 19922952 | tf_op jit(solution)/shard_map/jab,vujb->vuja/dot_general | solution.py:78
  255.3 3.9 copy.176
  259.2 53.9 %collective-permute-done.5 = f32[3,256,1024]{2,1,0:T(8,128)} collective-permute-done((f32[3,256,1024]{2,1,0:T(8,128)S(1)}, f32[3,256,1024]{2,1,0:T(8,128)}, u32[]{:S(2)}, u32[]{:S(2)}) %collective-permute-start.5) | collective-permute-done | bytes 3145760 | tf_op jit(solution)/shard_map/ppermute | solution.py:17
  313.0 5.3 %fusion.28 = f32[2,3,1024,128]{2,3,1,0:T(8,128)S(1)} fusion(f32[3,2,128,1024]{3,2,1,0:T(8,128)} %bitcast.82, f32[2,128,128]{1,2,0:T(8,128)} %copy.127, f32[2,128,128]{2,1,0:T(8,128)S(1)} %copy-done.43, pred[2]{0:T(512)(128)(4,1)S(1)} %copy-done.61), kind=kOutput, calls=%fused_computation.67 | convolution fusion | flops 1207992320 | bytes 6553602 | tf_op jit(solution)/shard_map/jab,vjbc->vjac/dot_general | solution.py:65
  318.4 5.4 %fusion.30 = f32[2,3,1024,128]{2,3,1,0:T(8,128)S(1)} fusion(f32[3,2,128,1024]{3,2,1,0:T(8,128)} %bitcast.80, f32[2,128,128]{1,2,0:T(8,128)S(1)} %copy-done.51, f32[2,128,128]{2,1,0:T(8,128)S(1)} %gather_fusion.6, pred[2]{0:T(512)(128)(4,1)S(1)} %copy-done.60), kind=kOutput, calls=%fused_computation.69 | convolution fusion | flops 1207992320 | bytes 6553602 | tf_op jit(solution)/shard_map/jab,vjbc->vjac/dot_general | solution.py:65
  323.8 6.3 %add_bitcast_fusion.1 = f32[3,2,128,1024]{3,2,0,1:T(8,128)S(1)} fusion(f32[2,3,1024,128]{2,3,1,0:T(8,128)S(1)} %fusion.28, f32[2,3,1024,128]{2,3,1,0:T(8,128)S(1)} %fusion.30, f32[2,3,1024,128]{2,3,1,0:T(8,128)S(1)} %copy-done.9, f32[2,3,1024,128]{2,3,1,0:T(8,128)S(1)} %copy-done.10, f32[3,2,128,1024]{3,2,1,0:T(8,128)} %bitcast.84, ...), kind=kOutput, calls=%fused_computation.82 | convolution fusion | flops 1211138048 | bytes 19136514 | tf_op jit(solution)/shard_map/jab,vjbc->vjac/dot_general | solution.py:65
  332.3 2.9 fusion.10
  335.2 5.2 %copy.180 = f32[3,256,1024]{1,0,2:T(4,128)} copy(f32[3,256,1024]{2,1,0:T(8,128)} %fusion.10) | data formatting | bytes 6291456 | tf_op jit(solution)/shard_map/add | solution.py:85
  340.4 21.3 %convolution_bitcast_fusion = f32[3,3]{1,0:T(4,128)S(1)} fusion(f32[3,256,1024]{1,0,2:T(4,128)} %copy.177, f32[3,256,1024]{1,0,2:T(4,128)} %copy.180), kind=kOutput, calls=%fused_computation.87 | convolution fusion | flops 28311552 | bytes 6291492 | tf_op jit(solution)/shard_map/vud,wud->vw/dot_general | solution.py:101
  361.7 34.6 %all-reduce.10 = (f32[3,3]{1,0:T(4,128)S(1)}, f32[3,3]{1,0:T(4,128)S(1)}) all-reduce(f32[3,3]{1,0:T(4,128)S(1)} %convolution_bitcast_fusion.1, f32[3,3]{1,0:T(4,128)S(1)} %convolution_bitcast_fusion), channel_id=1, replica_groups=mesh['real'=2,'up'=8,'dn'=2] {'up','dn'}, use_global_device_ids=true, to_apply=%region_0.1 | all-reduce | flops 18 | bytes 144 | tf_op jit(solution)/shard_map/psum | solution.py:98
  397.0 4.3 %broadcast_divide_fusion = f32[3,256,1024]{2,1,0:T(8,128)} fusion(f32[3,256,1024]{2,1,0:T(8,128)} %fusion.10, f32[3]{0:T(128)S(1)} %add_sqrt_fusion), kind=kLoop, calls=%fused_computation.83 | loop fusion | flops 786432 | bytes 6291468 | tf_op jit(solution)/shard_map/div | solution.py:108
  (234 shorter events, 37.6 us)
Async XLA Ops:
  0.6 19.0 %copy-start = (f32[16,128,128]{2,1,0:T(8,128)S(1)}, f32[16,128,128]{2,1,0:T(8,128)}, u32[]{:S(2)}) copy-start(f32[16,128,128]{2,1,0:T(8,128)} %param.27) | copy-start | bytes 3145732
  0.6 11.5 %copy-start.72 = (s32[8]{0:T(128)S(1)}, s32[8]{0:T(128)}, u32[]{:S(2)}) copy-start(s32[8]{0:T(128)} %constant.261) | copy-start | bytes 100
  0.7 12.2 %copy-start.71 = (s32[8]{0:T(128)S(1)}, s32[8]{0:T(128)}, u32[]{:S(2)}) copy-start(s32[8]{0:T(128)} %constant.258) | copy-start | bytes 100
  0.7 12.9 %copy-start.70 = (s32[8]{0:T(128)S(1)}, s32[8]{0:T(128)}, u32[]{:S(2)}) copy-start(s32[8]{0:T(128)} %constant.255) | copy-start | bytes 100
  0.7 11.5 %copy-start.2 = (s32[16,5]{0,1:T(8,128)S(1)}, s32[16,5]{0,1:T(8,128)}, u32[]{:S(2)}) copy-start(s32[16,5]{0,1:T(8,128)} %param.29) | copy-start | bytes 964
  0.7 14.9 %copy-start.3 = (s32[16,5]{0,1:T(8,128)S(1)}, s32[16,5]{0,1:T(8,128)}, u32[]{:S(2)}) copy-start(s32[16,5]{0,1:T(8,128)} %param.28) | copy-start | bytes 964
  0.7 137.5 %collective-permute-start.1 = (f32[3,256,1024]{2,1,0:T(8,128)}, f32[3,256,1024]{2,1,0:T(8,128)}, u32[]{:S(2)}, u32[]{:S(2)}) collective-permute-start(f32[3,256,1024]{2,1,0:T(8,128)} %param.23), channel_id=1, source_target_pairs={{0,4},{4,0},{2,6},{6,2},{8,12},{12,8},{10,14},{14,10},{1,5},{5,1},... | collective-permute-start | bytes 9437192 | tf_op jit(solution)/shard_map/ppermute | solution.py:17
  3.8 139.6 %collective-permute-start = (f32[3,256,1024]{2,1,0:T(8,128)}, f32[3,256,1024]{2,1,0:T(8,128)}, u32[]{:S(2)}, u32[]{:S(2)}) collective-permute-start(f32[3,256,1024]{2,1,0:T(8,128)} %param.23), channel_id=1, source_target_pairs={{0,2},{2,0},{4,6},{6,4},{8,10},{10,8},{12,14},{14,12},{1,3},{3,1},... | collective-permute-start | bytes 9437192 | tf_op jit(solution)/shard_map/ppermute | solution.py:17
  5.3 143.2 %collective-permute-start.2 = (f32[3,256,1024]{2,1,0:T(8,128)}, f32[3,256,1024]{2,1,0:T(8,128)}, u32[]{:S(2)}, u32[]{:S(2)}) collective-permute-start(f32[3,256,1024]{2,1,0:T(8,128)} %param.23), channel_id=1, source_target_pairs={{0,8},{8,0},{2,10},{10,2},{4,12},{12,4},{6,14},{14,6},{1,9},{9,1},... | collective-permute-start | bytes 9437192 | tf_op jit(solution)/shard_map/ppermute | solution.py:17
  11.5 5.4 %copy-start.69 = (s32[2]{0:T(128)S(1)}, s32[2]{0:T(128)}, u32[]{:S(2)}) copy-start(s32[2]{0:T(128)} %constant.244) | copy-start | bytes 28
  11.5 7.3 %copy-start.54 = (s32[256,14]{0,1:T(8,128)S(1)}, s32[256,14]{0,1:T(8,128)}, u32[]{:S(2)}) copy-start(s32[256,14]{0,1:T(8,128)} %param.24) | copy-start | bytes 43012
  11.5 7.3 %copy-start.58 = (f32[14]{0:T(128)S(1)}, f32[14]{0:T(128)}, u32[]{:S(2)}) copy-start(f32[14]{0:T(128)} %param.26) | copy-start | bytes 172
  11.5 85.9 %collective-permute-start.3 = (f32[3,256,1024]{1,2,0:T(8,128)}, f32[3,256,1024]{1,2,0:T(8,128)}, u32[]{:S(2)}, u32[]{:S(2)}) collective-permute-start(f32[3,256,1024]{1,2,0:T(8,128)} %copy.135), channel_id=1, source_target_pairs={{0,1},{1,0},{2,3},{3,2},{4,5},{5,4},{6,7},{7,6},{8,9},{9,8},{10,11... | collective-permute-start | bytes 9437192 | tf_op jit(solution)/shard_map/ppermute | solution.py:17
  14.2 6.8 %copy-start.53 = (s32[1024,14]{0,1:T(8,128)S(1)}, s32[1024,14]{0,1:T(8,128)}, u32[]{:S(2)}) copy-start(s32[1024,14]{0,1:T(8,128)} %param.25) | copy-start | bytes 172036
  16.9 44.7 %copy-start.55 = (s32[1024]{0:T(1024)}, s32[1024]{0:T(1024)S(1)}, u32[]{:S(2)}) copy-start(s32[1024]{0:T(1024)S(1)} %pad_clamp_fusion.12) | copy-start | bytes 12292
  20.2 7.7 %copy-start.20 = (f32[8,128,128]{2,1,0:T(8,128)}, f32[8,128,128]{2,1,0:T(8,128)S(1)}, u32[]{:S(2)}) copy-start(f32[8,128,128]{2,1,0:T(8,128)S(1)} %gather_fusion.12) | copy-start | bytes 1572868
  20.4 7.4 %copy-start.32 = (f32[8,128,128]{1,2,0:T(8,128)}, f32[8,128,128]{1,2,0:T(8,128)S(1)}, u32[]{:S(2)}) copy-start(f32[8,128,128]{1,2,0:T(8,128)S(1)} %copy.134) | copy-start | bytes 1572868
  21.1 6.8 %copy-start.48 = (f32[2,128,128]{1,2,0:T(8,128)}, f32[2,128,128]{1,2,0:T(8,128)S(1)}, u32[]{:S(2)}) copy-start(f32[2,128,128]{1,2,0:T(8,128)S(1)} %copy.119) | copy-start | bytes 393220
  21.3 6.6 %copy-start.5 = (f32[3,256,1024]{2,1,0:T(8,128)S(1)}, f32[3,256,1024]{2,1,0:T(8,128)}, u32[]{:S(2)}) copy-start(f32[3,256,1024]{2,1,0:T(8,128)} %param.23) | copy-start | bytes 9437188
  40.1 5.3 %copy-start.30 = (f32[8,128,128]{2,1,0:T(8,128)}, f32[8,128,128]{2,1,0:T(8,128)S(1)}, u32[]{:S(2)}) copy-start(f32[8,128,128]{2,1,0:T(8,128)S(1)} %gather_fusion.21) | copy-start | bytes 1572868
  50.4 5.3 %copy-start.24 = (f32[8,128,128]{2,1,0:T(8,128)}, f32[8,128,128]{2,1,0:T(8,128)S(1)}, u32[]{:S(2)}) copy-start(f32[8,128,128]{2,1,0:T(8,128)S(1)} %gather_fusion.18) | copy-start | bytes 1572868
  56.3 9.5 %copy-start.27 = (f32[8,128,128]{2,1,0:T(8,128)}, f32[8,128,128]{2,1,0:T(8,128)S(1)}, u32[]{:S(2)}) copy-start(f32[8,128,128]{2,1,0:T(8,128)S(1)} %gather_fusion.15) | copy-start | bytes 1572868
  57.9 7.9 %copy-start.22 = (f32[8,128,128]{2,1,0:T(8,128)}, f32[8,128,128]{2,1,0:T(8,128)S(1)}, u32[]{:S(2)}) copy-start(f32[8,128,128]{2,1,0:T(8,128)S(1)} %gather_fusion.23) | copy-start | bytes 1572868
  59.5 6.4 %copy-start.42 = (f32[2,128,128]{2,1,0:T(8,128)}, f32[2,128,128]{2,1,0:T(8,128)S(1)}, u32[]{:S(2)}) copy-start(f32[2,128,128]{2,1,0:T(8,128)S(1)} %gather_fusion.8) | copy-start | bytes 393220
  68.5 5.4 %copy-start.14 = (f32[8,3,256,128]{3,2,1,0:T(8,128)S(1)}, f32[8,3,256,128]{3,2,1,0:T(8,128)}, u32[]{:S(2)}) copy-start(f32[8,3,256,128]{3,2,1,0:T(8,128)} %gather_fusion.19) | copy-start | bytes 9437188
  68.5 5.4 %copy-start.31 = (f32[8,128,128]{2,1,0:T(8,128)S(1)}, f32[8,128,128]{2,1,0:T(8,128)}, u32[]{:S(2)}) copy-start(f32[8,128,128]{2,1,0:T(8,128)} %copy-done.30) | copy-start | bytes 1572868
  68.5 5.4 %copy-start.39 = (f32[8,128,128]{1,2,0:T(8,128)S(1)}, f32[8,128,128]{1,2,0:T(8,128)}, u32[]{:S(2)}) copy-start(f32[8,128,128]{1,2,0:T(8,128)} %copy.145) | copy-start | bytes 1572868
  68.5 5.5 %copy-start.63 = (pred[8]{0:T(512)(128)(4,1)S(1)}, pred[8]{0:T(512)(128)(4,1)}, u32[]{:S(2)}) copy-start(pred[8]{0:T(512)(128)(4,1)} %get-tuple-element.13) | copy-start | bytes 28
  80.6 16.8 %copy-start.17 = (f32[8,128,3,256]{3,1,2,0:T(8,128)S(1)}, f32[8,128,3,256]{3,1,2,0:T(8,128)}, u32[]{:S(2)}) copy-start(f32[8,128,3,256]{3,1,2,0:T(8,128)} %fusion.21) | copy-start | bytes 9437188
  80.6 16.8 %copy-start.23 = (f32[8,128,128]{2,1,0:T(8,128)S(1)}, f32[8,128,128]{2,1,0:T(8,128)}, u32[]{:S(2)}) copy-start(f32[8,128,128]{2,1,0:T(8,128)} %copy-done.22) | copy-start | bytes 1572868
  80.6 16.8 %copy-start.34 = (f32[8,128,128]{1,2,0:T(8,128)S(1)}, f32[8,128,128]{1,2,0:T(8,128)}, u32[]{:S(2)}) copy-start(f32[8,128,128]{1,2,0:T(8,128)} %copy.147) | copy-start | bytes 1572868
  80.6 16.8 %copy-start.56 = (pred[8]{0:T(512)(128)(4,1)S(1)}, pred[8]{0:T(512)(128)(4,1)}, u32[]{:S(2)}) copy-start(pred[8]{0:T(512)(128)(4,1)} %get-tuple-element.12) | copy-start | bytes 28
  148.6 6.4 %copy-start.40 = (f32[256,1024]{1,0:T(8,128)S(1)}, f32[256,1024]{1,0:T(8,128)}, u32[]{:S(2)}) copy-start(f32[256,1024]{1,0:T(8,128)} %fusion.49) | copy-start | bytes 3145732
  158.6 81.5 %collective-permute-start.7 = (f32[3,256,1024]{2,1,0:T(8,128)S(1)}, f32[3,256,1024]{2,1,0:T(8,128)}, u32[]{:S(2)}, u32[]{:S(2)}) collective-permute-start(f32[3,256,1024]{2,1,0:T(8,128)S(1)} %fusion.23), channel_id=1, source_target_pairs={{0,1},{1,0},{2,3},{3,2},{4,5},{5,4},{6,7},{7,6},{8,9},{9,8},{10,11... | collective-permute-start | bytes 9437192 | tf_op jit(solution)/shard_map/ppermute | solution.py:17
  177.5 135.5 %collective-permute-start.5 = (f32[3,256,1024]{2,1,0:T(8,128)S(1)}, f32[3,256,1024]{2,1,0:T(8,128)}, u32[]{:S(2)}, u32[]{:S(2)}) collective-permute-start(f32[3,256,1024]{2,1,0:T(8,128)S(1)} %fusion.23), channel_id=1, source_target_pairs={{0,4},{4,0},{2,6},{6,2},{8,12},{12,8},{10,14},{14,10},{1,5},{5,1},... | collective-permute-start | bytes 9437192 | tf_op jit(solution)/shard_map/ppermute | solution.py:17
  177.5 140.8 %collective-permute-start.4 = (f32[3,256,1024]{2,1,0:T(8,128)S(1)}, f32[3,256,1024]{2,1,0:T(8,128)}, u32[]{:S(2)}, u32[]{:S(2)}) collective-permute-start(f32[3,256,1024]{2,1,0:T(8,128)S(1)} %fusion.23), channel_id=1, source_target_pairs={{0,2},{2,0},{4,6},{6,4},{8,10},{10,8},{12,14},{14,12},{1,3},{3,1},... | collective-permute-start | bytes 9437192 | tf_op jit(solution)/shard_map/ppermute | solution.py:17
  180.2 143.6 %collective-permute-start.6 = (f32[3,256,1024]{2,1,0:T(8,128)S(1)}, f32[3,256,1024]{2,1,0:T(8,128)}, u32[]{:S(2)}, u32[]{:S(2)}) collective-permute-start(f32[3,256,1024]{2,1,0:T(8,128)S(1)} %fusion.23), channel_id=1, source_target_pairs={{0,8},{8,0},{2,10},{10,2},{4,12},{12,4},{6,14},{14,6},{1,9},{9,1},... | collective-permute-start | bytes 9437192 | tf_op jit(solution)/shard_map/ppermute | solution.py:17
  189.5 7.0 %copy-start.7 = (f32[3,256,1024]{1,2,0:T(8,128)S(1)}, f32[3,256,1024]{1,2,0:T(8,128)}, u32[]{:S(2)}) copy-start(f32[3,256,1024]{1,2,0:T(8,128)} %copy.163) | copy-start | bytes 9437188
  189.5 7.0 %copy-start.21 = (f32[8,128,128]{2,1,0:T(8,128)S(1)}, f32[8,128,128]{2,1,0:T(8,128)}, u32[]{:S(2)}) copy-start(f32[8,128,128]{2,1,0:T(8,128)} %copy-done.20) | copy-start | bytes 1572868
  189.5 7.0 %copy-start.33 = (f32[8,128,128]{1,2,0:T(8,128)S(1)}, f32[8,128,128]{1,2,0:T(8,128)}, u32[]{:S(2)}) copy-start(f32[8,128,128]{1,2,0:T(8,128)} %copy-done.32) | copy-start | bytes 1572868
  206.2 5.2 %copy-start.36 = (f32[8,128,128]{1,2,0:T(8,128)S(1)}, f32[8,128,128]{1,2,0:T(8,128)}, u32[]{:S(2)}) copy-start(f32[8,128,128]{1,2,0:T(8,128)} %copy.142) | copy-start | bytes 1572868
  255.3 57.8 %copy-start.43 = (f32[2,128,128]{2,1,0:T(8,128)S(1)}, f32[2,128,128]{2,1,0:T(8,128)}, u32[]{:S(2)}) copy-start(f32[2,128,128]{2,1,0:T(8,128)} %copy-done.42) | copy-start | bytes 393220
  255.3 57.8 %copy-start.61 = (pred[2]{0:T(512)(128)(4,1)S(1)}, pred[2]{0:T(512)(128)(4,1)}, u32[]{:S(2)}) copy-start(pred[2]{0:T(512)(128)(4,1)} %get-tuple-element.21) | copy-start | bytes 10
  313.0 5.3 %copy-start.51 = (f32[2,128,128]{1,2,0:T(8,128)S(1)}, f32[2,128,128]{1,2,0:T(8,128)}, u32[]{:S(2)}) copy-start(f32[2,128,128]{1,2,0:T(8,128)} %copy.124) | copy-start | bytes 393220
  313.0 5.3 %copy-start.60 = (pred[2]{0:T(512)(128)(4,1)S(1)}, pred[2]{0:T(512)(128)(4,1)}, u32[]{:S(2)}) copy-start(pred[2]{0:T(512)(128)(4,1)} %get-tuple-element.22) | copy-start | bytes 10
  318.3 5.4 %copy-start.9 = (f32[2,3,1024,128]{2,3,1,0:T(8,128)S(1)}, f32[2,3,1024,128]{2,3,1,0:T(8,128)}, u32[]{:S(2)}) copy-start(f32[2,3,1024,128]{2,3,1,0:T(8,128)} %fusion.32) | copy-start | bytes 9437188
  318.4 5.4 %copy-start.10 = (f32[2,3,1024,128]{2,3,1,0:T(8,128)S(1)}, f32[2,3,1024,128]{2,3,1,0:T(8,128)}, u32[]{:S(2)}) copy-start(f32[2,3,1024,128]{2,3,1,0:T(8,128)} %fusion.11) | copy-start | bytes 9437188
  318.4 5.4 %copy-start.47 = (f32[2,128,128]{1,2,0:T(8,128)S(1)}, f32[2,128,128]{1,2,0:T(8,128)}, u32[]{:S(2)}) copy-start(f32[2,128,128]{1,2,0:T(8,128)} %copy.130) | copy-start | bytes 393220
  (33 other events, 131.9 us)
where the time goes:
time: 409 us; the launch traced here: 402 us
  matrix products  162 us (40%)
  local copies, waits for them, and re-layouts  95.7 us (23%)
  waiting for transfers between devices  83.2 us (20%)
  blocking collectives  34.6 us (8%)
  starting transfers between devices  13.1 us (3%)
  other arithmetic  11.1 us (3%)
    ppermute x8, waiting for transfers between devices, swapped(): return lax.ppermute(block, axis, route)  83.2 us
    dot_general x6, matrix products, column_terms(): jnp.einsum('jab,vujb->vuja', pair_tiles(bank, table, rows, bit), blocks[:...  39.7 us
    psum x1, blocking collectives, body(): lax.psum((jnp.einsum('vud,wud->vw', first, first, precision=highest), jnp...  34.6 us
    dot_general x6, matrix products, up_swapped(): jnp.einsum('jab,vjbc->vjac', tiles, other.reshape(shape), precision=highest)  33.1 us
    gather x6, local copies, waits for them, and re-layouts, column_terms(): blocks[:, :, partner]  25.9 us
    dot_general x1, matrix products, body(): jnp.einsum('vud,wud->vw', first, second, precision=highest)  21.3 us
    dot_general x1, matrix products, body(): jnp.einsum('vud,wud->vw', first, first, precision=highest)  19.2 us
    gather x24, local copies, waits for them, and re-layouts, pair_tiles(): picked = bank[table[lower, bit + 1]]  16.6 us
  transfers between devices with their start and end apart: 8, of which 2 were waited for; matrix products, arithmetic and copies ran while one was open for 54% of the time, Pallas kernels for 0%

commit v1 on v0

--- a/solution.py
+++ b/solution.py
@@ -2,6 +2,8 @@
 import jax.numpy as jnp
 import numpy as np
 from jax import lax
+from jax.experimental import pallas as pl
+from jax.experimental.pallas import tpu as pltpu
 from jax.sharding import PartitionSpec as P
 
 highest = lax.Precision.HIGHEST
@@ -108,9 +110,314 @@
     return (second / scale[:, None, None], gram)
 
 
+MESH = pl.DeviceIdType.MESH
+HALF = 512
+ROWS = 256
+PAIRS = [(0, 0), (0, 1), (0, 2), (1, 1), (1, 2), (2, 2)]
+
+
+def split(value):
+    high = value.astype(jnp.bfloat16)
+    return high, (value - high.astype(jnp.float32)).astype(jnp.bfloat16)
+
+
+def product(a, b):
+    def dot(p, q):
+        return jnp.dot(p, q, preferred_element_type=jnp.float32)
+
+    return dot(a[0], b[0]) + (dot(a[1], b[0]) + dot(a[0], b[1]))
+
+
+def kernel(
+    x_ref, pay_ref, dn_ref, bank_ref, uidx_ref, didx_ref,
+    out_ref, stat_ref,
+    field, got, side, pot, xh, xl, uh, ul, dh, dl, urh, url, drh, drl,
+    rsend, rrecv, osend, orecv, bsend, brecv, psend, precv,
+):
+    x, up, core = lax.axis_index("real"), lax.axis_index("up"), lax.axis_index("dn")
+    z, y = up // 2, up % 2
+    h, low = z // 2, z % 2
+
+    def device(px, ph, plow=low, py=y, pc=core):
+        return (px, (ph * 2 + plow) * 2 + py, pc)
+
+    partners = [
+        device(x, h, pc=1 - core),
+        device(1 - x, h),
+        device(x, h, py=1 - y),
+        device(x, h, plow=1 - low),
+    ]
+    barrier = pltpu.get_barrier_semaphore()
+    for partner in partners + [device(x, 1 - h), device(1 - x, 1 - h)]:
+        pl.semaphore_signal(barrier, inc=1, device_id=partner, device_id_type=MESH)
+    pl.semaphore_wait(barrier, 6)
+
+    def remote(src, dst, send, recv, target):
+        return pltpu.make_async_remote_copy(
+            src_ref=src, dst_ref=dst, send_sem=send, recv_sem=recv,
+            device_id=target, device_id_type=MESH,
+        )
+
+    on_diagonal = x == h
+
+    def regroup(v):
+        rows = pl.ds(pl.multiple_of(h * ROWS, ROWS), ROWS)
+        near = x_ref.at[v, :, pl.ds(pl.multiple_of(h * HALF, HALF), HALF)]
+        far = x_ref.at[v, :, pl.ds(pl.multiple_of((1 - h) * HALF, HALF), HALF)]
+        dst = field.at[v, rows, :]
+        return (
+            pltpu.make_async_copy(near, dst, rrecv.at[v, 0]),
+            remote(near, dst, rsend.at[v, 0], rrecv.at[v, 0], device(h, x)),
+            remote(far, dst, rsend.at[v, 1], rrecv.at[v, 1], device(1 - h, x)),
+        )
+
+    def restore(v):
+        near = field.at[6 + v, pl.ds(pl.multiple_of(x * ROWS, ROWS), ROWS), :]
+        far = field.at[6 + v, pl.ds(pl.multiple_of((1 - x) * ROWS, ROWS), ROWS), :]
+        dst = out_ref.at[v, :, pl.ds(pl.multiple_of(x * HALF, HALF), HALF)]
+        return (
+            pltpu.make_async_copy(near, dst, brecv.at[v, 0]),
+            remote(near, dst, bsend.at[v, 0], brecv.at[v, 0], device(h, x)),
+            remote(far, dst, bsend.at[v, 1], brecv.at[v, 1], device(h, 1 - x)),
+        )
+
+    def start(copies):
+        own, near, far = copies
+
+        @pl.when(on_diagonal)
+        def _():
+            own.start()
+
+        @pl.when(jnp.logical_not(on_diagonal))
+        def _():
+            near.start()
+
+        far.start()
+
+    def finish(copies):
+        own, near, far = copies
+
+        @pl.when(on_diagonal)
+        def _():
+            own.wait()
+
+        @pl.when(jnp.logical_not(on_diagonal))
+        def _():
+            near.wait()
+
+        far.wait()
+
+    def exchange(t, d):
+        return remote(field.at[t], got.at[t, d], osend.at[t, d], orecv.at[t, d], partners[d])
+
+    side_copies = [
+        remote(pay_ref, side.at[0], psend.at[0], precv.at[0], device(x, 1 - h)),
+        remote(pay_ref, side.at[1], psend.at[1], precv.at[1], device(1 - x, h)),
+    ]
+    start(regroup(0))
+    for copy in side_copies:
+        copy.start()
+
+
+    def pair(table, r, k):
+        p = r ^ (1 << k)
+        first = r < p
+        tile = bank_ref[table[jnp.minimum(r, p) * table_width + k + 1]]
+        return jnp.where(first, tile, tile.T)
+
+    def own_tile(table, r):
+        tile = bank_ref[table[r * table_width]]
+        return 0.5 * (tile + tile.T)
+
+    table_width = 5
+    uh[...] = jnp.zeros_like(uh)
+    ul[...] = jnp.zeros_like(ul)
+    dh[...] = jnp.zeros_like(dh)
+    dl[...] = jnp.zeros_like(dl)
+    for ref in (urh, url, drh, drl):
+        ref[...] = jnp.zeros_like(ref)
+
+    def put(refs, index, value):
+        high, lo = split(value)
+        refs[0][index] = high
+        refs[1][index] = lo
+
+    def window(i):
+        return slice(i * 128, (i + 1) * 128)
+
+    for i in range(4):
+        r = (i // 2) * 8 + low * 4 + y * 2 + i % 2
+        put((uh, ul), (window(i), window(i)), own_tile(uidx_ref, r))
+        put((uh, ul), (window(i), window(i ^ 1)), pair(uidx_ref, r, 0))
+        put((uh, ul), (window(i), window(i ^ 2)), pair(uidx_ref, r, 3))
+        for d in range(2):
+            put((urh, url), (d, i // 2, window(i % 2), window(i % 2)), pair(uidx_ref, r, 1 + d))
+        q = core * 8 + x * 4 + i
+        put((dh, dl), (window(i), window(i)), own_tile(didx_ref, q))
+        put((dh, dl), (window(i), window(i ^ 1)), pair(didx_ref, q, 0))
+        put((dh, dl), (window(i), window(i ^ 2)), pair(didx_ref, q, 1))
+        for d in range(2):
+            put((drh, drl), (d, i // 2, window(i % 2), window(i % 2)), pair(didx_ref, q, 3 - d).T)
+
+    for copy in side_copies:
+        copy.wait()
+    mine, other = pay_ref[0:16, :], side[0, 0:16, :]
+    ups = jnp.concatenate(
+        [jnp.where(h == 0, mine, other), jnp.where(h == 0, other, mine)], axis=1
+    )
+    energy = jnp.where(on_diagonal, pay_ref[16:32, :], side[1, 16:32, :])
+    energy = jnp.concatenate([energy, energy], axis=1)
+    dns = dn_ref[:, pl.ds(pl.multiple_of(x * HALF, HALF), HALF)]
+    pot[...] = (
+        lax.dot_general(
+            ups, dns + energy, (((0,), (0,)), ((), ())),
+            precision=highest, preferred_element_type=jnp.float32,
+        )
+        + jnp.sum(energy * dns, axis=0, keepdims=True)
+        - 3.5
+    )
+
+    finish(regroup(0))
+    start(regroup(1))
+    for d in range(4):
+        exchange(0, d).start()
+
+    def local(t):
+        for rb in range(2):
+            rows = slice(rb * 256, rb * 256 + 256)
+            high, lo = split(field[t, rows, :])
+            xh[rows, :] = high
+            xl[rows, :] = lo
+        for rb in range(2):
+            rows = slice(rb * 256, rb * 256 + 256)
+            for cb in range(2):
+                cols = slice(cb * 256, cb * 256 + 256)
+                field[t + 3, rows, cols] = (
+                    pot[rows, cols] * field[t, rows, cols]
+                    + product((uh[rows, :], ul[rows, :]), (xh[:, cols], xl[:, cols]))
+                    + product((xh[rows, :], xl[rows, :]), (dh[:, cols], dl[:, cols]))
+                )
+
+    def from_dn(t, d):
+        for cb in range(2):
+            cols = slice(cb * 256, cb * 256 + 256)
+            for rb in range(2):
+                rows = slice(rb * 256, rb * 256 + 256)
+                field[t + 3, rows, cols] += product(
+                    split(got[t, d, rows, cols]), (drh[d, cb], drl[d, cb])
+                )
+
+    def from_up(t, d):
+        for rb in range(2):
+            rows = slice(rb * 256, rb * 256 + 256)
+            for cb in range(2):
+                cols = slice(cb * 256, cb * 256 + 256)
+                field[t + 3, rows, cols] += product(
+                    (urh[d - 2, rb], url[d - 2, rb]), split(got[t, d, rows, cols])
+                )
+
+    def step(t, carry):
+        @pl.when(t < 2)
+        def _():
+            finish(regroup(t + 1))
+
+            @pl.when(t < 1)
+            def _():
+                start(regroup(t + 2))
+
+            for d in range(4):
+                exchange(t + 1, d).start()
+
+        local(t)
+        for d in range(4):
+            exchange(t, d).wait()
+            (from_dn if d < 2 else from_up)(t, d)
+
+        @pl.when(t < 3)
+        def _():
+            for d in range(4):
+                exchange(t + 3, d).start()
+
+        @pl.when(t >= 3)
+        def _():
+            start(restore(t - 3))
+
+        return carry
+
+    lax.fori_loop(0, 6, step, 0)
+
+    def chunk(i, sums):
+        rows = pl.ds(pl.multiple_of(i * 16, 16), 16)
+        firsts = [field[3 + v, rows, :] for v in range(3)]
+        seconds = [field[6 + v, rows, :] for v in range(3)]
+        terms = [firsts[v] * firsts[w] for v, w in PAIRS]
+        terms += [firsts[v] * seconds[w] for v in range(3) for w in range(3)]
+        return [s + (term[0:8] + term[8:16]) for s, term in zip(sums, terms)]
+
+    sums = lax.fori_loop(0, HALF // 16, chunk, [jnp.zeros((8, HALF), jnp.float32)] * 15)
+    for i in range(15):
+        stat_ref[i : i + 1, :] = jnp.sum(sums[i], axis=0, keepdims=True)
+    stat_ref[15:16, :] = jnp.zeros((1, HALF), jnp.float32)
+    for v in range(3):
+        finish(restore(v))
+
+
+def fused(start, up_occupied, dn_occupied, disorder, hop_tiles, up_index, dn_index):
+    sites = up_occupied.shape[1]
+    up_part = jnp.pad(up_occupied.astype(jnp.float32).T, ((0, 16 - sites), (0, 0)))
+    dn_part = jnp.pad(dn_occupied.astype(jnp.float32).T, ((0, 16 - sites), (0, 0)))
+    energies = jnp.broadcast_to(jnp.pad(disorder, (0, 16 - sites))[:, None], (16, ROWS))
+    payload = jnp.concatenate([up_part, energies], axis=0)
+    vmem = pl.BlockSpec(memory_space=pltpu.VMEM)
+    smem = pl.BlockSpec(memory_space=pltpu.SMEM)
+    whole = pl.BlockSpec(memory_space=pl.ANY)
+    f32, b16, dma = jnp.float32, jnp.bfloat16, pltpu.SemaphoreType.DMA
+    second, stats = pl.pallas_call(
+        kernel,
+        out_shape=[
+            jax.ShapeDtypeStruct(start.shape, f32),
+            jax.ShapeDtypeStruct((16, HALF), f32),
+        ],
+        in_specs=[whole, vmem, vmem, vmem, smem, smem],
+        out_specs=[whole, vmem],
+        scratch_shapes=[
+            pltpu.VMEM((9, HALF, HALF), f32),
+            pltpu.VMEM((6, 4, HALF, HALF), f32),
+            pltpu.VMEM((2, 32, ROWS), f32),
+            pltpu.VMEM((HALF, HALF), f32),
+        ]
+        + [pltpu.VMEM((HALF, HALF), b16)] * 6
+        + [pltpu.VMEM((2, 2, 256, 256), b16)] * 4
+        + [dma((3, 2)), dma((3, 2)), dma((6, 4)), dma((6, 4)), dma((3, 2)), dma((3, 2)), dma((2,)), dma((2,))],
+        compiler_params=pltpu.CompilerParams(
+            collective_id=0, has_side_effects=True, vmem_limit_bytes=56 * 1024 * 1024
+        ),
+    )(start, payload, dn_part, hop_tiles, up_index.reshape(-1), dn_index.reshape(-1))
+    cells = start.shape[1] * start.shape[2] * lax.axis_size("up") * lax.axis_size("dn")
+    group = lax.axis_index("up") // 4
+    sums = jnp.sum(stats, axis=1)
+    sums = jnp.where(jnp.arange(2)[:, None] == group, sums[None, :], 0.0)
+    sums = lax.psum(sums, ("real", "up", "dn"))
+    sums = jnp.where(lax.axis_index("real") == 0, sums[0], sums[1])
+    correlation = sums[np.array([0, 1, 2, 1, 3, 4, 2, 4, 5])].reshape(3, 3)
+    image = sums[6:15].reshape(3, 3)
+    scale = jnp.sqrt(jnp.diagonal(correlation) / cells + 1e-06)
+    outer = scale[:, None] * scale[None, :]
+    gram = jnp.stack([correlation / outer, image / outer]) / cells
+    return (second / scale[:, None, None], gram)
+
+
+def route(start, *rest):
+    sizes = [lax.axis_size(axis) for axis in ("real", "up", "dn")]
+    fits = start.shape == (3, 256, 1024) and rest[3].shape == (16, 128, 128)
+    if sizes == [2, 8, 2] and fits and rest[0].shape[1] == 14:
+        return fused(start, *rest)
+    return body(start, *rest)
+
+
 def solution(mesh):
     return jax.shard_map(
-        body,
+        route,
         mesh=mesh,
         in_specs=(P("real", "up", "dn"), P("up", None), P("dn", None), P("real"), P(), P(), P()),
         out_specs=(P("real", "up", "dn"), P("real", None, None)),

time: 409 us -> 364 us (0.89); the launches traced: 402 us -> 362 us
  Pallas kernels: 0 us -> 296 us
  matrix products: 162 us -> 0 us
  local copies, waits for them, and re-layouts: 95.7 us -> 5.59 us
  waiting for transfers between devices: 83.2 us -> 0 us
  blocking collectives: 34.6 us -> 51.7 us
  starting transfers between devices: 13.1 us -> 0 us
    pallas_call x0 -> x1, Pallas kernels: none -> 296 us  [fused(): pl.pallas_call(kernel, out_shape=[jax.ShapeDtypeStruct(start.shape, f32),...]
    dot_general x25 -> x0, matrix products: 162 us -> none  [the longest x6 39.7 us: column_terms(): jnp.einsum('jab,vujb->vuja', pair_tiles(bank, table, rows, bit), blocks[:...]
    ppermute x8 -> x0, waiting for transfers between devices: 83.2 us -> none  [swapped(): return lax.ppermute(block, axis, route)]
    gather x39 -> x2, local copies, waits for them, and re-layouts: 52.7 us -> 1.32 us  [the longest x1 0.66 us: fused(): scale = jnp.sqrt(jnp.diagonal(correlation) / cells + 1e-06)]
    psum x1, blocking collectives: 34.6 us -> 51.7 us  [fused(): sums = lax.psum(sums, ('real', 'up', 'dn'))]
    add x7 -> x0, local copies, waits for them, and re-layouts: 15.8 us -> none  [the longest x3 11.2 us: operate(): return up_part + dn_part + (potential - shift)[None] * field]
    reshape x4 -> x5, local copies, waits for them, and re-layouts: 15 us -> 1.43 us  [the longest x1 0.6 us: fused(): up_index.reshape(-1)]
    ppermute x8 -> x0, starting transfers between devices: 13.1 us -> none  [swapped(): return lax.ppermute(block, axis, route)]
  transfers between devices with their start and end apart: 8 -> 0, of which waited for: 2 -> 0; matrix products, arithmetic and copies ran while one was open for 54% -> 0% of each run, Pallas kernels for 0% -> 0%
where the time goes in v1:
time: 364 us; the launch traced here: 362 us
  Pallas kernels  296 us (81%)
  blocking collectives  51.7 us (14%)
  other arithmetic  8.23 us (2%)
  local copies, waits for them, and re-layouts  5.59 us (2%)
    pallas_call x1, Pallas kernels, fused(): pl.pallas_call(kernel, out_shape=[jax.ShapeDtypeStruct(start.shape, f32),...  296 us
    psum x1, blocking collectives, fused(): sums = lax.psum(sums, ('real', 'up', 'dn'))  51.7 us

profile of v1, /device:TPU:0, one launch (start us, length us, event | category | flops | bytes accessed | tf_op | source)
XLA Modules:
  0.0 362.4 jit_solution(15285902144861927529)
XLA Ops:
  0.6 0.0 copy-start
  0.6 0.7 convert_bitcast_fusion.1
  1.4 0.7 compare_select_fusion
  2.1 0.7 select_maximum_fusion.pay_ref
  2.8 0.8 convert_bitcast_fusion
  3.6 0.6 pad.14.dn_ref
  4.3 0.8 copy.14
  5.0 0.6 reshape.147.uidx_ref
  5.6 0.8 copy.15
  6.4 0.6 reshape.148.didx_ref
  7.0 296.2 %shard_map.104 = (f32[3,256,1024]{2,1,0:T(8,128)}, f32[16,512]{1,0:T(8,128)}) custom-call(f32[3,256,1024]{2,1,0:T(8,128)} %x_ref.1, f32[32,256]{1,0:T(8,128)} %select_maximum_fusion.pay_ref, f32[16,1024]{1,0:T(8,128)} %pad.14.dn_ref, f32[16,128,128]{2,1,0:T(8,128)} %bank_ref.1, s32[80]{0:T(128)} %reshape.147.uidx_ref, s32[80]{0:T(128)} %reshape.148.didx_ref), custom_call_target="tpu_custom_call" | custom-call | tf_op jit(solution)/shard_map/pallas_call | solution.py:375
  303.2 0.9 reduce_sum.9
  304.0 0.1 broadcast_select_fusion
  304.1 51.7 %psum.7 = f32[2,16]{1,0:T(2,128)S(1)} all-reduce(f32[2,16]{1,0:T(2,128)S(1)} %broadcast_select_fusion), channel_id=1, replica_groups=mesh['real'=2,'up'=8,'dn'=2] {'real','up','dn'}, use_global_device_ids=true, to_apply=%region_1.2 | all-reduce | flops 32 | bytes 256 | tf_op jit(solution)/shard_map/psum | solution.py:400
  355.8 0.0 copy-done
  355.8 0.7 gather_fusion
  356.5 0.1 reshape.149
  356.6 0.7 gather_fusion.1
  357.3 4.2 %broadcast_divide_fusion = f32[3,256,1024]{2,1,0:T(8,128)} fusion(f32[3,256,1024]{2,1,0:T(8,128)} %get-tuple-element.4, f32[3]{0:T(128)S(1)} %add_sqrt_fusion), kind=kLoop, calls=%fused_computation.2 | loop fusion | flops 786432 | bytes 6291468 | tf_op jit(solution)/shard_map/div | solution.py:407
  361.5 0.1 reshape.150
  361.5 0.1 slice_reduce_fusion
  361.6 0.1 reshape.151
  361.7 0.1 multiply_divide_fusion.1
  361.8 0.6 copy.16
  (7 shorter events, 0.0 us)
Async XLA Ops:
  0.6 355.2 %copy-start = (s32[9]{0:T(128)S(1)}, s32[9]{0:T(128)}, u32[]{:S(2)}) copy-start(s32[9]{0:T(128)} %constant.71) | copy-start | bytes 112

commit v2 on v1

--- a/solution.py
+++ b/solution.py
@@ -113,6 +113,8 @@
 MESH = pl.DeviceIdType.MESH
 HALF = 512
 ROWS = 256
+PARTS = 2
+PART = ROWS // PARTS
 PAIRS = [(0, 0), (0, 1), (0, 2), (1, 1), (1, 2), (2, 2)]
 
 
@@ -132,7 +134,7 @@
     x_ref, pay_ref, dn_ref, bank_ref, uidx_ref, didx_ref,
     out_ref, stat_ref,
     field, got, side, pot, xh, xl, uh, ul, dh, dl, urh, url, drh, drl,
-    rsend, rrecv, osend, orecv, bsend, brecv, psend, precv,
+    hop, rsend, rrecv, rown, hrecv, osend, orecv, bsend, brecv, bown, psend, precv, given, taken, gsend, grecv,
 ):
     x, up, core = lax.axis_index("real"), lax.axis_index("up"), lax.axis_index("dn")
     z, y = up // 2, up % 2
@@ -147,10 +149,11 @@
         device(x, h, py=1 - y),
         device(x, h, plow=1 - low),
     ]
+    beside, across = device(1 - x, h), device(x, 1 - h)
     barrier = pltpu.get_barrier_semaphore()
-    for partner in partners + [device(x, 1 - h), device(1 - x, 1 - h)]:
+    for partner in partners + [across]:
         pl.semaphore_signal(barrier, inc=1, device_id=partner, device_id_type=MESH)
-    pl.semaphore_wait(barrier, 6)
+    pl.semaphore_wait(barrier, 5)
 
     def remote(src, dst, send, recv, target):
         return pltpu.make_async_remote_copy(
@@ -160,52 +163,105 @@
 
     on_diagonal = x == h
 
-    def regroup(v):
-        rows = pl.ds(pl.multiple_of(h * ROWS, ROWS), ROWS)
-        near = x_ref.at[v, :, pl.ds(pl.multiple_of(h * HALF, HALF), HALF)]
-        far = x_ref.at[v, :, pl.ds(pl.multiple_of((1 - h) * HALF, HALF), HALF)]
-        dst = field.at[v, rows, :]
-        return (
-            pltpu.make_async_copy(near, dst, rrecv.at[v, 0]),
-            remote(near, dst, rsend.at[v, 0], rrecv.at[v, 0], device(h, x)),
-            remote(far, dst, rsend.at[v, 1], rrecv.at[v, 1], device(1 - h, x)),
-        )
-
-    def restore(v):
-        near = field.at[6 + v, pl.ds(pl.multiple_of(x * ROWS, ROWS), ROWS), :]
-        far = field.at[6 + v, pl.ds(pl.multiple_of((1 - x) * ROWS, ROWS), ROWS), :]
-        dst = out_ref.at[v, :, pl.ds(pl.multiple_of(x * HALF, HALF), HALF)]
-        return (
-            pltpu.make_async_copy(near, dst, brecv.at[v, 0]),
-            remote(near, dst, bsend.at[v, 0], brecv.at[v, 0], device(h, x)),
-            remote(far, dst, bsend.at[v, 1], brecv.at[v, 1], device(h, 1 - x)),
-        )
-
-    def start(copies):
-        own, near, far = copies
-
+    def part(c):
+        return slice(c * PART, (c + 1) * PART)
+
+    def to_half(i):
+        return pl.ds(pl.multiple_of(i * HALF, HALF), HALF)
+
+    def to_rows(i, c=0, count=ROWS):
+        return pl.ds(pl.multiple_of(i * ROWS + c * PART, PART), count)
+
+    class Regroup:
+        def __init__(self, v):
+            near = x_ref.at[v, :, to_half(h)]
+            self.own = lambda: pltpu.make_async_copy(
+                near, field.at[v, to_rows(h), :], rown.at[v]
+            )
+            self.far = lambda: remote(
+                x_ref.at[v, :, to_half(1 - h)], field.at[v, to_rows(h), :],
+                rsend.at[v, PARTS], rrecv.at[v, PARTS], device(1 - h, x),
+            )
+            self.hops = lambda: [
+                remote(
+                    x_ref.at[v, part(c), to_half(h)], hop.at[v, part(c), :],
+                    rsend.at[v, c], hrecv.at[v, c], beside,
+                )
+                for c in range(PARTS)
+            ]
+            self.relays = lambda: [
+                remote(
+                    hop.at[v, part(c), :], field.at[v, to_rows(h, c, PART), :],
+                    rsend.at[v, c], rrecv.at[v, c], across,
+                )
+                for c in range(PARTS)
+            ]
+
+    class Restore:
+        def __init__(self, v):
+            self.own = lambda: pltpu.make_async_copy(
+                field.at[6 + v, to_rows(x), :], out_ref.at[v, :, to_half(x)], bown.at[v]
+            )
+            self.far = lambda: remote(
+                field.at[6 + v, to_rows(1 - x), :], out_ref.at[v, :, to_half(x)],
+                bsend.at[v, PARTS], brecv.at[v, PARTS], device(h, 1 - x),
+            )
+            self.hops = lambda: [
+                remote(
+                    field.at[6 + v, to_rows(x, c, PART), :], hop.at[3 + v, part(c), :],
+                    bsend.at[v, c], hrecv.at[3 + v, c], across,
+                )
+                for c in range(PARTS)
+            ]
+            self.relays = lambda: [
+                remote(
+                    hop.at[3 + v, part(c), :], out_ref.at[v, part(c), to_half(x)],
+                    bsend.at[v, c], brecv.at[v, c], beside,
+                )
+                for c in range(PARTS)
+            ]
+
+    def launch(move):
         @pl.when(on_diagonal)
         def _():
-            own.start()
+            move.own().start()
 
         @pl.when(jnp.logical_not(on_diagonal))
         def _():
-            near.start()
-
-        far.start()
-
-    def finish(copies):
-        own, near, far = copies
-
+            for copy in move.hops():
+                copy.start()
+
+        move.far().start()
+
+    def relay(move):
         @pl.when(on_diagonal)
         def _():
-            own.wait()
+            for first, second in zip(move.hops(), move.relays()):
+                first.wait_recv()
+                second.start()
+
+    def arrive(move):
+        @pl.when(on_diagonal)
+        def _():
+            move.own().wait()
 
         @pl.when(jnp.logical_not(on_diagonal))
         def _():
-            near.wait()
-
-        far.wait()
+            for copy in move.relays():
+                copy.wait_recv()
+
+        move.far().wait_recv()
+
+    def drain(move):
+        @pl.when(on_diagonal)
+        def _():
+            for copy in move.relays():
+                copy.wait_send()
+
+        @pl.when(jnp.logical_not(on_diagonal))
+        def _():
+            for copy in move.hops():
+                copy.wait_send()
 
     def exchange(t, d):
         return remote(field.at[t], got.at[t, d], osend.at[t, d], orecv.at[t, d], partners[d])
@@ -214,7 +270,7 @@
         remote(pay_ref, side.at[0], psend.at[0], precv.at[0], device(x, 1 - h)),
         remote(pay_ref, side.at[1], psend.at[1], precv.at[1], device(1 - x, h)),
     ]
-    start(regroup(0))
+    launch(Regroup(0))
     for copy in side_copies:
         copy.start()
 
@@ -277,8 +333,10 @@
         - 3.5
     )
 
-    finish(regroup(0))
-    start(regroup(1))
+    relay(Regroup(0))
+    Regroup(0).far().wait_send()
+    launch(Regroup(1))
+    arrive(Regroup(0))
     for d in range(4):
         exchange(0, d).start()
 
@@ -319,16 +377,23 @@
     def step(t, carry):
         @pl.when(t < 2)
         def _():
-            finish(regroup(t + 1))
+            relay(Regroup(t + 1))
+            Regroup(t + 1).far().wait_send()
 
             @pl.when(t < 1)
             def _():
-                start(regroup(t + 2))
-
+                launch(Regroup(t + 2))
+
+            arrive(Regroup(t + 1))
             for d in range(4):
                 exchange(t + 1, d).start()
 
         local(t)
+
+        @pl.when(t >= 4)
+        def _():
+            relay(Restore(t - 4))
+
         for d in range(4):
             exchange(t, d).wait()
             (from_dn if d < 2 else from_up)(t, d)
@@ -340,7 +405,7 @@
 
         @pl.when(t >= 3)
         def _():
-            start(restore(t - 3))
+            launch(Restore(t - 3))
 
         return carry
 
@@ -356,10 +421,28 @@
 
     sums = lax.fori_loop(0, HALF // 16, chunk, [jnp.zeros((8, HALF), jnp.float32)] * 15)
     for i in range(15):
-        stat_ref[i : i + 1, :] = jnp.sum(sums[i], axis=0, keepdims=True)
-    stat_ref[15:16, :] = jnp.zeros((1, HALF), jnp.float32)
+        line = jnp.sum(sums[i], axis=0, keepdims=True)
+        line = (line[:, 0:128] + line[:, 128:256]) + (line[:, 256:384] + line[:, 384:512])
+        given[0, i : i + 1, :] = line
+    given[0, 15:16, :] = jnp.zeros((1, 128), jnp.float32)
+
+    def add(k, target):
+        copy = remote(given.at[k], taken.at[k], gsend.at[k], grecv.at[k], target)
+        copy.start()
+        copy.wait()
+
+    for k in range(4):
+        add(k, partners[k])
+        given[k + 1] = given[k] + taken[k]
+        if k == 0:
+            relay(Restore(2))
+    add(4, across)
+    stat_ref[...] = jnp.where(on_diagonal, given[4], taken[4])
     for v in range(3):
-        finish(restore(v))
+        arrive(Restore(v))
+        drain(Restore(v))
+        Restore(v).far().wait_send()
+        drain(Regroup(v))
 
 
 def fused(start, up_occupied, dn_occupied, disorder, hop_tiles, up_index, dn_index):
@@ -376,7 +459,7 @@
         kernel,
         out_shape=[
             jax.ShapeDtypeStruct(start.shape, f32),
-            jax.ShapeDtypeStruct((16, HALF), f32),
+            jax.ShapeDtypeStruct((16, 128), f32),
         ],
         in_specs=[whole, vmem, vmem, vmem, smem, smem],
         out_specs=[whole, vmem],
@@ -388,17 +471,17 @@
         ]
         + [pltpu.VMEM((HALF, HALF), b16)] * 6
         + [pltpu.VMEM((2, 2, 256, 256), b16)] * 4
-        + [dma((3, 2)), dma((3, 2)), dma((6, 4)), dma((6, 4)), dma((3, 2)), dma((3, 2)), dma((2,)), dma((2,))],
+        + [pltpu.VMEM((6, ROWS, HALF), f32)]
+        + [dma((3, PARTS + 1)), dma((3, PARTS + 1)), dma((3,)), dma((6, PARTS))]
+        + [dma((6, 4)), dma((6, 4))]
+        + [dma((3, PARTS + 1)), dma((3, PARTS + 1)), dma((3,)), dma((2,)), dma((2,))]
+        + [pltpu.VMEM((5, 16, 128), f32), pltpu.VMEM((5, 16, 128), f32), dma((5,)), dma((5,))],
         compiler_params=pltpu.CompilerParams(
             collective_id=0, has_side_effects=True, vmem_limit_bytes=56 * 1024 * 1024
         ),
     )(start, payload, dn_part, hop_tiles, up_index.reshape(-1), dn_index.reshape(-1))
     cells = start.shape[1] * start.shape[2] * lax.axis_size("up") * lax.axis_size("dn")
-    group = lax.axis_index("up") // 4
     sums = jnp.sum(stats, axis=1)
-    sums = jnp.where(jnp.arange(2)[:, None] == group, sums[None, :], 0.0)
-    sums = lax.psum(sums, ("real", "up", "dn"))
-    sums = jnp.where(lax.axis_index("real") == 0, sums[0], sums[1])
     correlation = sums[np.array([0, 1, 2, 1, 3, 4, 2, 4, 5])].reshape(3, 3)
     image = sums[6:15].reshape(3, 3)
     scale = jnp.sqrt(jnp.diagonal(correlation) / cells + 1e-06)

time: 364 us -> 293 us (0.80)
  blocking collectives: 51.7 us -> 0 us
  Pallas kernels: 296 us -> 278 us
    psum x1 -> x0, blocking collectives: 51.7 us -> none  [fused(): sums = lax.psum(sums, ('real', 'up', 'dn'))]
    pallas_call x1, Pallas kernels: 296 us -> 278 us  [fused(): pl.pallas_call(kernel, out_shape=[jax.ShapeDtypeStruct(start.shape, f32),...]
where the time goes in v2:
time: 293 us; the launch traced here: 292 us
  Pallas kernels  278 us (95%)
  other arithmetic  8.08 us (3%)
  local copies, waits for them, and re-layouts  5.58 us (2%)
    pallas_call x1, Pallas kernels, fused(): pl.pallas_call(kernel, out_shape=[jax.ShapeDtypeStruct(start.shape, f32),...  278 us

profile of v2, /device:TPU:0, one launch (start us, length us, event | category | flops | bytes accessed | tf_op | source)
XLA Modules:
  0.0 292.4 jit_solution(10748378859959205391)
XLA Ops:
  0.6 0.0 copy-start
  0.6 0.7 convert_bitcast_fusion.1
  1.4 0.7 compare_select_fusion
  2.1 0.7 select_maximum_fusion.pay_ref
  2.8 0.8 convert_bitcast_fusion
  3.6 0.6 pad.14.dn_ref
  4.3 0.8 copy.14
  5.0 0.6 reshape.137.uidx_ref
  5.6 0.8 copy.15
  6.4 0.6 reshape.138.didx_ref
  7.0 278.0 %shard_map.104 = (f32[3,256,1024]{2,1,0:T(8,128)}, f32[16,128]{1,0:T(8,128)}) custom-call(f32[3,256,1024]{2,1,0:T(8,128)} %x_ref.1, f32[32,256]{1,0:T(8,128)} %select_maximum_fusion.pay_ref, f32[16,1024]{1,0:T(8,128)} %pad.14.dn_ref, f32[16,128,128]{2,1,0:T(8,128)} %bank_ref.1, s32[80]{0:T(128)} %reshape.137.uidx_ref, s32[80]{0:T(128)} %reshape.138.didx_ref), custom_call_target="tpu_custom_call" | custom-call | tf_op jit(solution)/shard_map/pallas_call | solution.py:458
  285.0 0.8 reduce_sum.9
  285.8 0.0 copy-done
  285.8 0.7 gather_fusion
  286.5 0.1 reshape.139
  286.6 0.7 gather_fusion.1
  287.3 4.2 %broadcast_divide_fusion = f32[3,256,1024]{2,1,0:T(8,128)} fusion(f32[3,256,1024]{2,1,0:T(8,128)} %get-tuple-element.4, f32[3]{0:T(128)S(1)} %add_sqrt_fusion), kind=kLoop, calls=%fused_computation.2 | loop fusion | flops 786432 | bytes 6291468 | tf_op jit(solution)/shard_map/div | solution.py:490
  291.5 0.1 reshape.140
  291.5 0.1 slice.3
  291.6 0.1 reshape.141
  291.7 0.1 multiply_divide_fusion.1
  291.8 0.6 copy.16
  (4 shorter events, 0.0 us)
Async XLA Ops:
  0.6 285.2 %copy-start = (s32[9]{0:T(128)S(1)}, s32[9]{0:T(128)}, u32[]{:S(2)}) copy-start(s32[9]{0:T(128)} %constant.45) | copy-start | bytes 112
